TPU v7x, 32 devices: a whole 2x2x4 slice. The times are simulated.
32 devices in a mesh: pair: 4 (over z), intg: 8 (over y, x, core).
Axes of the slice: x: 2, y: 2, z: 4, core: 2. Of those that a mesh axis runs over, the one named last changes fastest.
Arguments:
- amplitudes: bfloat16 [1536, 8192], P('pair', 'intg'), may hold values from -6 to 6
- integrals: bfloat16 [4096, 8192], P('pair', 'intg'), may hold values from -0.125 to 0.125
- sym_rows: int32 [32], P('pair'), may hold values from 0 to 3
- sym_cols: int32 [64], P('intg'), may hold values from 0 to 3
- mirror_rows: int32 [4096], replicated, may hold values from 0 to 4095, as said below
Outputs:
- residual: bfloat16 [1536, 4096], P('intg', 'pair')
Inputs may be any that keep to these rules, and one draw needn't show every extreme that they name: `mirror_rows`: an involution without fixed points; it maps the rows of each 128-row tile onto all rows of one other tile.
All inputs are finite; a program needn't handle non-finite values.
Results may differ from a plain program's by a relative error of at most 0.001.
Values may be sent and summed in bfloat16 or wider, within the bound.
A program may use at most 128 MiB of HBM per device.

v0:
```python
import jax
import jax.numpy as jnp
from jax import lax
from jax.sharding import PartitionSpec as P


def contract_pair(left, right):
    return lax.dot_general(
        left, right, (((1,), (1,)), ((), ())), preferred_element_type=jnp.float32
    )


def shards(amplitudes, integrals, sym_rows, sym_cols, mirror_rows):
    tile_rows = integrals.shape[0] // sym_rows.shape[0]
    row_sym = jnp.repeat(sym_rows, tile_rows)
    col_sym = jnp.repeat(sym_cols, tile_rows)
    masked = jnp.where(row_sym[:, None] == col_sym[None, :], integrals, jnp.zeros((), jnp.bfloat16))
    ab_rows = integrals.shape[0]
    own_twins = lax.dynamic_slice_in_dim(mirror_rows, lax.axis_index("pair") * ab_rows, ab_rows, 0)
    partial_sums = contract_pair(lax.all_gather(amplitudes, "pair", axis=0, tiled=True), masked)
    result_block = lax.psum_scatter(partial_sums, "intg", scatter_dimension=0, tiled=True)
    all_columns = lax.all_gather(result_block, "pair", axis=1, tiled=True)
    result_block = result_block - jnp.take(all_columns, own_twins, axis=1)
    return result_block.astype(jnp.bfloat16)


def solution(mesh):
    return jax.shard_map(
        shards,
        mesh=mesh,
        in_specs=(P("pair", "intg"), P("pair", "intg"), P("pair"), P("intg"), P()),
        out_specs=P("intg", "pair"),
        check_vma=False,
    )
```

profile of v0, /device:TPU:0, one launch (start us, length us, event | category | flops | bytes accessed | tf_op | source)
XLA Modules:
  0.0 247.7 jit_solution(17519875900810251594)
XLA Ops:
  6.5 0.0 all-gather.3.cloned.1.call-start
  6.5 0.7 all-gather.3.cloned.1.call-update
  7.3 0.0 reduce-scatter.4.cloned.1.call-start
  7.3 0.7 broadcast_bitcast_fusion
  8.0 67.1 %all-gather.3.cloned.1.call-done = bf16[1536,1024]{1,0:T(8,128)(2,1)} async-done(((bf16[384,1024]{1,0:T(8,128)(2,1)}), bf16[1536,1024]{1,0:T(8,128)(2,1)}) %all-gather.3.cloned.1.call-update) | async-done | bytes 3145744 | tf_op jit(solution)/shard_map/all_gather | solution.py:20
  75.2 8.6 %convolution_bitcast_fusion = f32[1536,1024]{0,1:T(8,128)} fusion(bf16[1536,1024]{1,0:T(8,128)(2,1)} %all-gather.3.cloned.1.call-done, bf16[1024,1024]{1,0:T(8,128)(2,1)} %param.6, s32[1024]{0:T(1024)S(1)} %get-tuple-element.5, s32[1024]{0:T(1024)S(1)} %get-tuple-element.6), kind=kOutput, calls=%fused_computation.1 | convolution fusion | flops 3223322624 | bytes 11542528 | tf_op jit(solution)/shard_map/dot_general | solution.py:8
  83.8 6.6 %copy.8 = f32[1536,1024]{1,0:T(8,128)} copy(f32[1536,1024]{0,1:T(8,128)} %convolution_bitcast_fusion) | data formatting | bytes 12582912
  90.4 0.0 copy-start.1
  90.4 0.0 reduce-scatter.4.cloned.1.call-update
  90.4 0.0 all-gather.5.cloned.1.call-start
  90.4 60.5 %reduce-scatter.4.cloned.1.call-done = f32[192,1024]{1,0:T(8,128)} async-done(((f32[1536,1024]{1,0:T(8,128)}), f32[192,1024]{1,0:T(8,128)}) %reduce-scatter.4.cloned.1.call-update) | async-done | bytes 786448
  150.9 2.4 copy.9
  153.4 0.0 all-gather.5.cloned.1.call-update
  153.4 0.0 copy-done.1
  153.5 0.0 copy-start
  153.5 80.8 %all-gather.5.cloned.1.call-done = f32[192,4096]{0,1:T(8,128)} async-done(((f32[192,1024]{0,1:T(8,128)}), f32[192,4096]{0,1:T(8,128)}) %all-gather.5.cloned.1.call-update) | async-done | bytes 3145744 | tf_op jit(solution)/shard_map/all_gather | solution.py:22
  234.3 5.6 %gather_fusion = f32[1024,192]{1,0:T(8,128)S(1)} fusion(f32[192,4096]{0,1:T(8,128)} %all-gather.5.cloned.1.call-done, s32[1024]{0:T(1024)S(1)} %fusion.4), kind=kCustom, calls=%fused_computation | custom fusion | bytes 1576960 | tf_op jit(solution)/shard_map/jit(_take)/gather | solution.py:23
  240.0 0.0 copy-done
  240.0 0.2 fusion.2
  240.2 0.9 copy.7
  (2 shorter events, 0.0 us)
Async XLA Ops:
  6.5 68.6 %all-gather.3.cloned.1.call-start = ((), (), s32[]{:S(2)}) async-start(), calls=%async_computation.1 | async-start | bytes 3932160 | tf_op jit(solution)/shard_map/all_gather | solution.py:20
  7.3 143.7 %reduce-scatter.4.cloned.1.call-start = ((), (), s32[]{:S(2)}) async-start(), calls=%async_computation.3 | async-start | bytes 7077888
  90.4 63.0 %copy-start.1 = (s32[4096]{0:T(1024)S(1)}, s32[4096]{0:T(1024)}, u32[]{:S(2)}) copy-start(s32[4096]{0:T(1024)} %param.9) | copy-start | bytes 49156
  90.4 143.9 %all-gather.5.cloned.1.call-start = ((), (), s32[]{:S(2)}) async-start(), calls=%async_computation.2 | async-start | bytes 5242880 | tf_op jit(solution)/shard_map/all_gather | solution.py:22
  153.5 86.5 %copy-start = (f32[192,1024]{0,1:T(8,128)S(1)}, f32[192,1024]{0,1:T(8,128)}, u32[]{:S(2)}) copy-start(f32[192,1024]{0,1:T(8,128)} %copy.9) | copy-start | bytes 2359300
Sparse Core Ops, SparseCore 0:
  8.9 66.1 all-gather.2
  90.5 60.3 reduce-scatter.3
  153.5 80.7 all-gather.4
where the time goes:
time: 248 us
  waiting for transfers between devices  209 us (84%)
  local copies, waits for them, and re-layouts  16.3 us (7%)
  between operations  13.2 us (5%)
  matrix products  8.65 us (3%)
    all_gather x1, waiting for transfers between devices, shards(): all_columns = lax.all_gather(result_block, 'pair', axis=1, tiled=True)  80.8 us
    all_gather x1, waiting for transfers between devices, shards(): lax.all_gather(amplitudes, 'pair', axis=0, tiled=True)  67.1 us
    unnamed x4, waiting for transfers between devices  61.2 us
    unnamed x6, local copies, waits for them, and re-layouts  9 us
    dot_general x1, matrix products, contract_pair(): lax.dot_general(left, right, (((1,), (1,)), ((), ())), preferred_element_...  8.65 us
    gather x1, local copies, waits for them, and re-layouts, shards(): result_block = result_block - jnp.take(all_columns, own_twins, axis=1)  5.65 us
  transfers between devices with their start and end apart: 3, of which 3 were waited for; matrix products, arithmetic and copies ran while one was open for 0% of the time, Pallas kernels for 0%

commit v1 on v0

--- a/solution.py
+++ b/solution.py
@@ -1,7 +1,16 @@
+import functools
+
 import jax
 import jax.numpy as jnp
 from jax import lax
+from jax.experimental import pallas as pl
+from jax.experimental.pallas import tpu as pltpu
 from jax.sharding import PartitionSpec as P
+
+MESH = pl.DeviceIdType.MESH
+PARTS = 2
+CORES = 2
+SIDE = 2
 
 
 def contract_pair(left, right):
@@ -10,7 +19,7 @@
     )
 
 
-def shards(amplitudes, integrals, sym_rows, sym_cols, mirror_rows):
+def shards_plain(amplitudes, integrals, sym_rows, sym_cols, mirror_rows):
     tile_rows = integrals.shape[0] // sym_rows.shape[0]
     row_sym = jnp.repeat(sym_rows, tile_rows)
     col_sym = jnp.repeat(sym_cols, tile_rows)
@@ -24,9 +33,423 @@
     return result_block.astype(jnp.bfloat16)
 
 
+def ladder_kernel(
+    planes, tiles, tile,
+    t_ref, v_ref, mask_ref, turn_ref, pick_ref, out_ref,
+    v_in, turned, tall, prod, from_core, hop_one, hop_two, cont, from_left, from_right, slots,
+    v_sem, t_recv, t_right, t_left, core_send, core_recv,
+    a_send, a_recv, b_send, b_recv, a2_send, a2_recv, b2_send, b2_recv,
+    zr_send, zr_recv, zl_send, zl_recv, gr_send, gl_send, g_recv,
+):
+    parts, rows, depth = t_ref.shape[1], t_ref.shape[2], t_ref.shape[3]
+    columns = prod.shape[-1]
+    half = columns // 2
+    group = cont.shape[-1]
+    per_plane = group // tile
+    last = planes - 1
+    p = lax.axis_index("pair")
+    g = lax.axis_index("intg")
+    core, x, y = g % 2, (g // 2) % 2, g // 4
+    chip = g // 2
+    sibling = g + 1 - 2 * core
+    x_peer = g + 2 - 4 * x
+    y_peer = g + 4 - 8 * y
+    low, high = slice(0, half), slice(half, columns)
+
+    def order(step):
+        result = jnp.int32(0)
+        for plane in range(planes):
+            near = sorted(range(planes), key=lambda q: abs(q - plane))
+            for at, q in enumerate(near):
+                result = result + jnp.where(jnp.logical_and(p == plane, step == at), q, 0)
+        return result
+
+    load_v = pltpu.make_async_copy(v_ref, v_in, v_sem)
+    load_v.start()
+
+    barrier = pltpu.get_barrier_semaphore()
+    for peer in (sibling, x_peer, y_peer):
+        pl.semaphore_signal(barrier, inc=1, device_id={"intg": peer}, device_id_type=MESH)
+
+    @pl.when(p > 0)
+    def _():
+        pl.semaphore_signal(barrier, inc=1, device_id={"pair": p - 1}, device_id_type=MESH)
+
+    @pl.when(p < last)
+    def _():
+        pl.semaphore_signal(barrier, inc=1, device_id={"pair": p + 1}, device_id_type=MESH)
+
+    ends = (p == 0).astype(jnp.int32) + (p == last).astype(jnp.int32)
+    pl.semaphore_wait(barrier, 5 - ends)
+
+    def remote(src, dst, send, recv, **where):
+        return pltpu.make_async_remote_copy(
+            src_ref=src, dst_ref=dst, send_sem=send, recv_sem=recv,
+            device_id=where, device_id_type=MESH,
+        )
+
+    def t_copy(src, q, c, send, plane):
+        return remote(src, tall.at[q, :, c], send.at[q, c], t_recv.at[q, c], pair=plane)
+
+    def own_t(c):
+        @pl.when(p < last)
+        def _():
+            t_copy(t_ref.at[:, c], p, c, t_right, p + 1).start()
+
+        @pl.when(p > 0)
+        def _():
+            t_copy(t_ref.at[:, c], p, c, t_left, p - 1).start()
+
+    own_t(0)
+
+    load_v.wait()
+    for t in range(tiles):
+        span = slice(t * tile, (t + 1) * tile)
+        kept = v_in[span, :] * mask_ref[t : t + 1, :]
+        turned[span, :] = jnp.dot(
+            turn_ref[t], kept, preferred_element_type=jnp.float32
+        ).astype(jnp.bfloat16)
+
+    def core_copy(q, c):
+        return remote(
+            prod.at[q, 1 - core, c], from_core.at[q, c],
+            core_send.at[q, c], core_recv.at[q, c], intg=sibling,
+        )
+
+    def a_copy(q, c):
+        return remote(prod.at[q, core, c, :, low], hop_one.at[q, c, :, low],
+                      a_send.at[q, c], a_recv.at[q, c], intg=x_peer)
+
+    def b_copy(q, c):
+        return remote(prod.at[q, core, c, :, high], hop_one.at[q, c, :, high],
+                      b_send.at[q, c], b_recv.at[q, c], intg=y_peer)
+
+    def a2_copy(q, c):
+        return remote(prod.at[q, core, c, :, low], hop_two.at[c, :, low],
+                      a2_send.at[c], a2_recv.at[c], intg=y_peer)
+
+    def b2_copy(q, c):
+        return remote(prod.at[q, core, c, :, high], hop_two.at[c, :, high],
+                      b2_send.at[c], b2_recv.at[c], intg=x_peer)
+
+    events = planes * parts
+
+    def multiply(n):
+        c, at = n // planes, n % planes
+        q = order(at)
+
+        @pl.when(at == 0)
+        def _():
+            tall[q, :, c] = t_ref[:, c]
+
+        @pl.when(at > 0)
+        def _():
+            t_copy(t_ref.at[:, c], q, c, t_right, p).wait_recv()
+
+            @pl.when(jnp.logical_and(q < p, p < last))
+            def _():
+                t_copy(tall.at[q, :, c], q, c, t_right, p + 1).start()
+
+            @pl.when(jnp.logical_and(q > p, p > 0))
+            def _():
+                t_copy(tall.at[q, :, c], q, c, t_left, p - 1).start()
+
+        @pl.when(jnp.logical_and(at == 1, c + 1 < parts))
+        def _():
+            own_t(c + 1)
+
+        left = tall[q, :, c].reshape(CORES * rows, depth)
+        wide = min(256, columns)
+
+        def block(i, _):
+            span = pl.ds(pl.multiple_of(i * wide, wide), wide)
+            prod[q, :, c, :, span] = contract_pair(left, turned[span, :]).reshape(CORES, rows, wide)
+            return 0
+
+        lax.fori_loop(0, columns // wide, block, 0)
+        core_copy(q, c).start()
+
+    def add_cores(n):
+        c, q = n // planes, order(n % planes)
+        core_copy(q, c).wait_recv()
+        prod[q, core, c] = prod[q, core, c] + from_core[q, c]
+
+        @pl.when(q % 2 != x)
+        def _():
+            a_copy(q, c).start()
+
+        @pl.when(q // 2 != y)
+        def _():
+            b_copy(q, c).start()
+
+    def add_first(n):
+        c, q = n // planes, order(n % planes)
+
+        @pl.when(q % 2 == x)
+        def _():
+            a_copy(q, c).wait_recv()
+            prod[q, core, c, :, low] = prod[q, core, c, :, low] + hop_one[q, c, :, low]
+
+            @pl.when(q // 2 != y)
+            def _():
+                a2_copy(q, c).start()
+
+        @pl.when(q // 2 == y)
+        def _():
+            b_copy(q, c).wait_recv()
+            prod[q, core, c, :, high] = prod[q, core, c, :, high] + hop_one[q, c, :, high]
+
+            @pl.when(q % 2 != x)
+            def _():
+                b2_copy(q, c).start()
+
+    def event(n, _):
+        @pl.when(n < events)
+        def _():
+            multiply(n)
+
+        @pl.when(jnp.logical_and(n >= 1, n < events + 1))
+        def _():
+            add_cores(n - 1)
+
+        @pl.when(n >= 2)
+        def _():
+            add_first(n - 2)
+
+        return 0
+
+    lax.fori_loop(0, events + 2, event, 0)
+
+    def right_sum(q, c):
+        return remote(cont.at[q, c], from_left.at[q, c], zr_send.at[q, c], zr_recv.at[q, c], pair=p + 1)
+
+    def left_sum(q, c):
+        return remote(cont.at[q, c], from_right.at[q, c], zl_send.at[q, c], zl_recv.at[q, c], pair=p - 1)
+
+    def collect(c):
+        a2_copy(chip, c).wait_recv()
+        b2_copy(chip, c).wait_recv()
+        prod[chip, core, c] = prod[chip, core, c] + hop_two[c]
+
+        def fill(q):
+            for s in range(per_plane):
+                def term(t, total):
+                    span = pl.ds(pl.multiple_of(t * tile, tile), tile)
+                    scale = pick_ref[(q * per_plane + s) * tiles + t]
+                    return total + scale * prod[chip, core, c, :, span]
+
+                cont[q, c, :, s * tile : (s + 1) * tile] = lax.fori_loop(
+                    0, tiles, term, jnp.zeros((rows, tile), jnp.float32))
+
+        for away in range(last, 0, -1):
+            @pl.when(p + away <= last)
+            def _():
+                q = p + away
+                fill(q)
+
+                @pl.when(p > 0)
+                def _():
+                    right_sum(q, c).wait_recv()
+                    cont[q, c] = cont[q, c] + from_left[q, c]
+
+                right_sum(q, c).start()
+
+            @pl.when(p - away >= 0)
+            def _():
+                q = p - away
+                fill(q)
+
+                @pl.when(p < last)
+                def _():
+                    left_sum(q, c).wait_recv()
+                    cont[q, c] = cont[q, c] + from_right[q, c]
+
+                left_sum(q, c).start()
+        fill(p)
+
+    def right_slot(q, c):
+        return remote(slots.at[q, c], slots.at[q, c], gr_send.at[q, c], g_recv.at[q, c], pair=p + 1)
+
+    def left_slot(q, c):
+        return remote(slots.at[q, c], slots.at[q, c], gl_send.at[q, c], g_recv.at[q, c], pair=p - 1)
+
+    def settle(c):
+        @pl.when(p > 0)
+        def _():
+            right_sum(p, c).wait_recv()
+            cont[p, c] = cont[p, c] + from_left[p, c]
+
+        @pl.when(p < last)
+        def _():
+            left_sum(p, c).wait_recv()
+            cont[p, c] = cont[p, c] + from_right[p, c]
+
+        slots[p, c] = cont[p, c].astype(jnp.bfloat16)
+
+        @pl.when(p < last)
+        def _():
+            right_slot(p, c).start()
+
+        @pl.when(p > 0)
+        def _():
+            left_slot(p, c).start()
+
+    def pass_on(c):
+        for away in range(1, planes):
+            @pl.when(p - away >= 0)
+            def _():
+                q = p - away
+                right_slot(q, c).wait_recv()
+
+                @pl.when(p < last)
+                def _():
+                    right_slot(q, c).start()
+
+            @pl.when(p + away <= last)
+            def _():
+                q = p + away
+                left_slot(q, c).wait_recv()
+
+                @pl.when(p > 0)
+                def _():
+                    left_slot(q, c).start()
+
+    def emit(c):
+        def one(t, _):
+            total = jnp.zeros((rows, tile), jnp.float32)
+            for q in range(planes):
+                for s in range(per_plane):
+                    scale = pick_ref[(q * per_plane + s) * tiles + t]
+                    total = total + scale * slots[q, c, :, s * tile : (s + 1) * tile].astype(jnp.float32)
+            span = pl.ds(pl.multiple_of(t * tile, tile), tile)
+            out_ref[c * rows : (c + 1) * rows, span] = jnp.dot(
+                total.astype(jnp.bfloat16), turn_ref[t], preferred_element_type=jnp.float32
+            ).astype(jnp.bfloat16)
+            return 0
+
+        lax.fori_loop(0, tiles, one, 0)
+
+    for c in range(parts):
+        collect(c)
+    for c in range(parts):
+        settle(c)
+    for c in range(parts):
+        pass_on(c)
+        emit(c)
+
+    def drain(n, _):
+        c, q = n // planes, n % planes
+        core_copy(q, c).wait_send()
+
+        @pl.when(q % 2 != x)
+        def _():
+            a_copy(q, c).wait_send()
+
+        @pl.when(q // 2 != y)
+        def _():
+            b_copy(q, c).wait_send()
+
+        @pl.when(jnp.logical_and(q % 2 == x, q // 2 != y))
+        def _():
+            a2_copy(q, c).wait_send()
+
+        @pl.when(jnp.logical_and(q % 2 != x, q // 2 == y))
+        def _():
+            b2_copy(q, c).wait_send()
+
+        @pl.when(jnp.logical_and(q <= p, p < last))
+        def _():
+            t_copy(tall.at[q, :, c], q, c, t_right, p + 1).wait_send()
+            right_slot(q, c).wait_send()
+
+        @pl.when(jnp.logical_and(q >= p, p > 0))
+        def _():
+            t_copy(tall.at[q, :, c], q, c, t_left, p - 1).wait_send()
+            left_slot(q, c).wait_send()
+
+        @pl.when(q > p)
+        def _():
+            right_sum(q, c).wait_send()
+
+        @pl.when(q < p)
+        def _():
+            left_sum(q, c).wait_send()
+
+        return 0
+
+    lax.fori_loop(0, events, drain, 0)
+
+
+def shards(planes, amplitudes, integrals, sym_rows, sym_cols, mirror_rows):
+    tiles = sym_rows.shape[0]
+    columns, depth = integrals.shape
+    tile = columns // tiles
+    all_tiles = mirror_rows.shape[0] // tile
+    count = all_tiles // 2
+    per_plane = count // planes
+    rows = amplitudes.shape[0] // (CORES * PARTS)
+
+    mask = (sym_rows[:, None] == jnp.repeat(sym_cols, tile)[None, :]).astype(jnp.bfloat16)
+    twin = mirror_rows.reshape(all_tiles, tile)
+    partner = twin[:, 0] // tile
+    here = jnp.arange(all_tiles, dtype=jnp.int32)
+    leads = here < partner
+    first = jnp.minimum(here, partner)
+    rank = jnp.sum((leads[None, :]) & (here[None, :] < first[:, None]), axis=1).astype(jnp.int32)
+    start = lax.axis_index("pair") * tiles
+    own_twin = lax.dynamic_slice_in_dim(twin, start, tiles, 0) % tile
+    own_leads = lax.dynamic_slice_in_dim(leads, start, tiles, 0)
+    own_rank = lax.dynamic_slice_in_dim(rank, start, tiles, 0)
+    lane = jnp.arange(tile, dtype=jnp.int32)
+    spot = jnp.where(own_leads[:, None], lane[None, :], own_twin)
+    sign = jnp.where(own_leads, 1.0, -1.0).astype(jnp.bfloat16)
+    turn = jnp.where(lane[None, :, None] == spot[:, None, :], sign[:, None, None], jnp.zeros((), jnp.bfloat16))
+    pick = (jnp.arange(count, dtype=jnp.int32)[:, None] == own_rank[None, :]).astype(jnp.float32).reshape(-1)
+
+    dma = pltpu.SemaphoreType.DMA
+    grid = (planes, PARTS)
+    vmem = pl.BlockSpec(memory_space=pltpu.VMEM)
+    group = per_plane * tile
+    return pl.pallas_call(
+        functools.partial(ladder_kernel, planes, tiles, tile),
+        out_shape=jax.ShapeDtypeStruct((PARTS * rows, columns), jnp.bfloat16),
+        in_specs=[vmem, pl.BlockSpec(memory_space=pl.ANY), vmem, vmem, pl.BlockSpec(memory_space=pltpu.SMEM)],
+        out_specs=vmem,
+        scratch_shapes=[
+            pltpu.VMEM((columns, depth), jnp.bfloat16),
+            pltpu.VMEM((columns, depth), jnp.bfloat16),
+            pltpu.VMEM((planes, CORES, PARTS, rows, depth), jnp.bfloat16),
+            pltpu.VMEM((planes, CORES, PARTS, rows, columns), jnp.float32),
+            pltpu.VMEM((planes, PARTS, rows, columns), jnp.float32),
+            pltpu.VMEM((planes, PARTS, rows, columns), jnp.float32),
+            pltpu.VMEM((PARTS, rows, columns), jnp.float32),
+            pltpu.VMEM((planes, PARTS, rows, group), jnp.float32),
+            pltpu.VMEM((planes, PARTS, rows, group), jnp.float32),
+            pltpu.VMEM((planes, PARTS, rows, group), jnp.float32),
+            pltpu.VMEM((planes, PARTS, rows, group), jnp.bfloat16),
+            dma,
+            dma(grid), dma(grid), dma(grid), dma(grid), dma(grid),
+            dma(grid), dma(grid), dma(grid), dma(grid),
+            dma((PARTS,)), dma((PARTS,)), dma((PARTS,)), dma((PARTS,)),
+            dma(grid), dma(grid), dma(grid), dma(grid),
+            dma(grid), dma(grid), dma(grid),
+        ],
+        compiler_params=pltpu.CompilerParams(
+            collective_id=0, has_side_effects=True, vmem_limit_bytes=48 * 1024 * 1024
+        ),
+        cost_estimate=pl.CostEstimate(
+            flops=2 * planes * amplitudes.shape[0] * columns * depth,
+            bytes_accessed=2 * (amplitudes.size + integrals.size), transcendentals=0,
+        ),
+    )(amplitudes.reshape(CORES, PARTS, rows, depth), integrals, mask, turn, pick)
+
+
 def solution(mesh):
+    planes, chips = mesh.shape["pair"], mesh.shape["intg"] // CORES
+    direct = planes == chips and chips == SIDE * SIDE
+    body = functools.partial(shards, planes) if direct else shards_plain
     return jax.shard_map(
-        shards,
+        body,
         mesh=mesh,
         in_specs=(P("pair", "intg"), P("pair", "intg"), P("pair"), P("intg"), P()),
         out_specs=P("intg", "pair"),

time: 248 us -> 124 us (0.50)
  waiting for transfers between devices: 209 us -> 0 us
  Pallas kernels: 0 us -> 117 us
  between operations: 13.2 us -> 0.03 us
  local copies, waits for them, and re-layouts: 16.3 us -> 3.71 us
  matrix products: 8.65 us -> 0 us
  other arithmetic: 0.23 us -> 2.76 us
    all_gather x2 -> x0, waiting for transfers between devices: 148 us -> none  [the longest x1 80.8 us: shards(): all_columns = lax.all_gather(result_block, 'pair', axis=1, tiled=True)]
    pallas_call x0 -> x1, Pallas kernels: none -> 117 us  [shards(): pl.pallas_call(functools.partial(ladder_kernel, planes, tiles, tile), out...]
    unnamed x4 -> x0, waiting for transfers between devices: 61.2 us -> none
    dot_general x1 -> x0, matrix products: 8.65 us -> none  [contract_pair(): lax.dot_general(left, right, (((1,), (1,)), ((), ())), preferred_element_...]
    gather x1 -> x0, local copies, waits for them, and re-layouts: 5.65 us -> none  [shards(): result_block = result_block - jnp.take(all_columns, own_twins, axis=1)]
    unnamed x6 -> x7, local copies, waits for them, and re-layouts: 9 us -> 3.47 us
  transfers between devices with their start and end apart: 3 -> 0, of which waited for: 3 -> 0; matrix products, arithmetic and copies ran while one was open for 0% -> 0% of each run, Pallas kernels for 0% -> 0%
where the time goes in v1:
time: 124 us; the launch traced here: 123 us
  Pallas kernels  117 us (94%)
  local copies, waits for them, and re-layouts  3.71 us (3%)
  other arithmetic  2.76 us (2%)
    pallas_call x1, Pallas kernels, shards(): pl.pallas_call(functools.partial(ladder_kernel, planes, tiles, tile), out...  117 us
    unnamed x7, local copies, waits for them, and re-layouts  3.47 us

profile of v1, /device:TPU:0, one launch (start us, length us, event | category | flops | bytes accessed | tf_op | source)
XLA Modules:
  0.0 123.3 jit_solution(4401573433805829953)
XLA Ops:
  0.0 0.0 copy-start
  0.0 0.9 fusion.3
  0.9 0.2 convert_reduce_fusion
  1.1 0.1 dynamic_slice.11
  1.1 0.1 select_convert_fusion
  1.2 0.8 fusion.8
  2.0 0.0 copy-done
  2.0 0.1 broadcast_bitcast_fusion
  2.1 0.1 reshape.53.pick_ref
  2.1 0.7 compare_convert_fusion.mask_ref
  2.9 0.1 fusion.turn_ref
  3.0 0.0 copy-start.1
  3.0 1.6 %copy-done.1 = bf16[1024,1024]{1,0:T(8,128)(2,1)S(1)} copy-done((bf16[1024,1024]{1,0:T(8,128)(2,1)S(1)}, bf16[1024,1024]{1,0:T(8,128)(2,1)}, u32[]{:S(2)}) %copy-start.1) | copy-done | bytes 2097176
  4.6 0.0 copy-start.2
  4.6 1.1 copy-done.2
  5.7 116.8 %shard_map.55 = bf16[192,1024]{1,0:T(8,128)(2,1)S(1)} custom-call(bf16[2,2,96,1024]{3,2,1,0:T(8,128)(2,1)S(1)} %bitcast.4, bf16[1024,1024]{1,0:T(8,128)(2,1)S(1)} %copy-done.1, bf16[8,1024]{1,0:T(8,128)(2,1)S(1)} %compare_convert_fusion.mask_ref, bf16[8,128,128]{2,1,0:T(8,128)(2,1)S(1)} %fusion.turn_ref, f32[128]{0:T(128)S(1)} %reshape.53.pick_ref), custom_call_target="tpu_custom_call" | custom-call | flops 3221225472 | bytes 2883584 | tf_op jit(solution)/shard_map/pallas_call | solution.py:413
  122.6 0.7 copy.8
  (2 shorter events, 0.0 us)
Async XLA Ops:
  0.0 2.0 %copy-start = (s32[8]{0:T(128)S(1)}, s32[8]{0:T(128)}, u32[]{:S(2)}) copy-start(s32[8]{0:T(128)} %param.8) | copy-start | bytes 100
  3.0 1.6 %copy-start.1 = (bf16[1024,1024]{1,0:T(8,128)(2,1)S(1)}, bf16[1024,1024]{1,0:T(8,128)(2,1)}, u32[]{:S(2)}) copy-start(bf16[1024,1024]{1,0:T(8,128)(2,1)} %v_ref.1) | copy-start | bytes 6291460
  4.6 1.1 copy-start.2

commit v2 on v1

--- a/solution.py
+++ b/solution.py
@@ -8,7 +8,8 @@
 from jax.sharding import PartitionSpec as P
 
 MESH = pl.DeviceIdType.MESH
-PARTS = 2
+PARTS = 4
+LAG = 3
 CORES = 2
 SIDE = 2
 
@@ -35,9 +36,9 @@
 
 def ladder_kernel(
     planes, tiles, tile,
-    t_ref, v_ref, mask_ref, turn_ref, pick_ref, out_ref,
-    v_in, turned, tall, prod, from_core, hop_one, hop_two, cont, from_left, from_right, slots,
-    v_sem, t_recv, t_right, t_left, core_send, core_recv,
+    t_ref, v_ref, rows_ref, cols_ref, mirror_ref, twin_ref, out_ref,
+    rank_ref, turn, v_in, turned, tall, prod, from_core, hop_one, hop_two, cont, from_left, from_right, slots,
+    v_sem, own_sem, t_recv, t_right, t_left, core_send, core_recv,
     a_send, a_recv, b_send, b_recv, a2_send, a2_recv, b2_send, b2_recv,
     zr_send, zr_recv, zl_send, zl_recv, gr_send, gl_send, g_recv,
 ):
@@ -66,6 +67,8 @@
 
     load_v = pltpu.make_async_copy(v_ref, v_in, v_sem)
     load_v.start()
+    load_t = pltpu.make_async_copy(t_ref, tall.at[p], own_sem)
+    load_t.start()
 
     barrier = pltpu.get_barrier_semaphore()
     for peer in (sibling, x_peer, y_peer):
@@ -102,13 +105,37 @@
 
     own_t(0)
 
+    all_tiles = planes * tiles
+    base = p * tiles
+    partners = [mirror_ref[u * tile] // tile for u in range(all_tiles)]
     load_v.wait()
-    for t in range(tiles):
-        span = slice(t * tile, (t + 1) * tile)
-        kept = v_in[span, :] * mask_ref[t : t + 1, :]
+
+    def prepare(t, _):
+        at = base + t
+        partner = mirror_ref[at * tile] // tile
+        leads = at < partner
+        first = jnp.minimum(at, partner)
+        rank = jnp.int32(0)
+        for u in range(all_tiles):
+            rank = rank + jnp.where(jnp.logical_and(u < partners[u], u < first), 1, 0)
+        rank_ref[t] = rank
+        lane = lax.broadcasted_iota(jnp.int32, (1, tile), 1)
+        spot = jnp.where(leads, lane, twin_ref[pl.ds(at, 1), :] - partner * tile)
+        sign = jnp.where(leads, 1.0, -1.0)
+        row = lax.broadcasted_iota(jnp.int32, (tile, tile), 0)
+        turn[t] = jnp.where(row == spot, sign, 0.0).astype(jnp.bfloat16)
+        span = pl.ds(pl.multiple_of(t * tile, tile), tile)
+        for u in range(depth // tile):
+            keep = jnp.where(rows_ref[t] == cols_ref[u], 1.0, 0.0)
+            lanes = slice(u * tile, (u + 1) * tile)
+            v_in[span, lanes] = (v_in[span, lanes].astype(jnp.float32) * keep).astype(jnp.bfloat16)
         turned[span, :] = jnp.dot(
-            turn_ref[t], kept, preferred_element_type=jnp.float32
+            turn[t], v_in[span, :], preferred_element_type=jnp.float32
         ).astype(jnp.bfloat16)
+        return 0
+
+    lax.fori_loop(0, tiles, prepare, 0)
+    load_t.wait()
 
     def core_copy(q, c):
         return remote(
@@ -138,10 +165,6 @@
         c, at = n // planes, n % planes
         q = order(at)
 
-        @pl.when(at == 0)
-        def _():
-            tall[q, :, c] = t_ref[:, c]
-
         @pl.when(at > 0)
         def _():
             t_copy(t_ref.at[:, c], q, c, t_right, p).wait_recv()
@@ -203,69 +226,53 @@
             def _():
                 b2_copy(q, c).start()
 
-    def event(n, _):
-        @pl.when(n < events)
-        def _():
-            multiply(n)
-
-        @pl.when(jnp.logical_and(n >= 1, n < events + 1))
-        def _():
-            add_cores(n - 1)
-
-        @pl.when(n >= 2)
-        def _():
-            add_first(n - 2)
-
-        return 0
-
-    lax.fori_loop(0, events + 2, event, 0)
-
     def right_sum(q, c):
         return remote(cont.at[q, c], from_left.at[q, c], zr_send.at[q, c], zr_recv.at[q, c], pair=p + 1)
 
     def left_sum(q, c):
         return remote(cont.at[q, c], from_right.at[q, c], zl_send.at[q, c], zl_recv.at[q, c], pair=p - 1)
+
+    def pick(k, t):
+        return jnp.where(rank_ref[t] == k, 1.0, 0.0)
 
     def collect(c):
         a2_copy(chip, c).wait_recv()
         b2_copy(chip, c).wait_recv()
         prod[chip, core, c] = prod[chip, core, c] + hop_two[c]
 
-        def fill(q):
-            for s in range(per_plane):
-                def term(t, total):
-                    span = pl.ds(pl.multiple_of(t * tile, tile), tile)
-                    scale = pick_ref[(q * per_plane + s) * tiles + t]
-                    return total + scale * prod[chip, core, c, :, span]
-
-                cont[q, c, :, s * tile : (s + 1) * tile] = lax.fori_loop(
-                    0, tiles, term, jnp.zeros((rows, tile), jnp.float32))
-
-        for away in range(last, 0, -1):
-            @pl.when(p + away <= last)
-            def _():
-                q = p + away
-                fill(q)
-
-                @pl.when(p > 0)
-                def _():
-                    right_sum(q, c).wait_recv()
-                    cont[q, c] = cont[q, c] + from_left[q, c]
-
-                right_sum(q, c).start()
-
-            @pl.when(p - away >= 0)
-            def _():
-                q = p - away
-                fill(q)
-
-                @pl.when(p < last)
-                def _():
-                    left_sum(q, c).wait_recv()
-                    cont[q, c] = cont[q, c] + from_right[q, c]
-
-                left_sum(q, c).start()
-        fill(p)
+        def fill(k, _):
+            total = jnp.zeros((rows, tile), jnp.float32)
+            for t in range(tiles):
+                total = total + pick(k, t) * prod[chip, core, c, :, t * tile : (t + 1) * tile]
+            span = pl.ds(pl.multiple_of(k % per_plane * tile, tile), tile)
+            cont[k // per_plane, c, :, span] = total
+            return 0
+
+        lax.fori_loop(0, planes * per_plane, fill, 0)
+        send_sums(c, last)
+
+    def send_sums(c, away):
+        @pl.when(p + away <= last)
+        def _():
+            q = p + away
+
+            @pl.when(p > 0)
+            def _():
+                right_sum(q, c).wait_recv()
+                cont[q, c] = cont[q, c] + from_left[q, c]
+
+            right_sum(q, c).start()
+
+        @pl.when(p - away >= 0)
+        def _():
+            q = p - away
+
+            @pl.when(p < last)
+            def _():
+                left_sum(q, c).wait_recv()
+                cont[q, c] = cont[q, c] + from_right[q, c]
+
+            left_sum(q, c).start()
 
     def right_slot(q, c):
         return remote(slots.at[q, c], slots.at[q, c], gr_send.at[q, c], g_recv.at[q, c], pair=p + 1)
@@ -294,48 +301,70 @@
         def _():
             left_slot(p, c).start()
 
-    def pass_on(c):
-        for away in range(1, planes):
-            @pl.when(p - away >= 0)
-            def _():
-                q = p - away
-                right_slot(q, c).wait_recv()
-
-                @pl.when(p < last)
-                def _():
-                    right_slot(q, c).start()
-
-            @pl.when(p + away <= last)
-            def _():
-                q = p + away
-                left_slot(q, c).wait_recv()
-
-                @pl.when(p > 0)
-                def _():
-                    left_slot(q, c).start()
+    def pass_on(c, away):
+        @pl.when(p - away >= 0)
+        def _():
+            q = p - away
+            right_slot(q, c).wait_recv()
+
+            @pl.when(p < last)
+            def _():
+                right_slot(q, c).start()
+
+        @pl.when(p + away <= last)
+        def _():
+            q = p + away
+            left_slot(q, c).wait_recv()
+
+            @pl.when(p > 0)
+            def _():
+                left_slot(q, c).start()
 
     def emit(c):
         def one(t, _):
             total = jnp.zeros((rows, tile), jnp.float32)
             for q in range(planes):
                 for s in range(per_plane):
-                    scale = pick_ref[(q * per_plane + s) * tiles + t]
+                    scale = pick(q * per_plane + s, t)
                     total = total + scale * slots[q, c, :, s * tile : (s + 1) * tile].astype(jnp.float32)
             span = pl.ds(pl.multiple_of(t * tile, tile), tile)
-            out_ref[c * rows : (c + 1) * rows, span] = jnp.dot(
-                total.astype(jnp.bfloat16), turn_ref[t], preferred_element_type=jnp.float32
+            out_ref[pl.ds(pl.multiple_of(c * rows, rows), rows), span] = jnp.dot(
+                total.astype(jnp.bfloat16), turn[t], preferred_element_type=jnp.float32
             ).astype(jnp.bfloat16)
             return 0
 
         lax.fori_loop(0, tiles, one, 0)
 
-    for c in range(parts):
-        collect(c)
-    for c in range(parts):
-        settle(c)
-    for c in range(parts):
-        pass_on(c)
-        emit(c)
+    stages = [collect]
+    stages += [functools.partial(send_sums, away=away) for away in range(last - 1, 0, -1)]
+    stages += [settle]
+    stages += [functools.partial(pass_on, away=away) for away in range(1, planes)]
+    stages += [emit]
+
+    def event(n, _):
+        @pl.when(n < events)
+        def _():
+            multiply(n)
+
+        @pl.when(jnp.logical_and(n >= 1, n < events + 1))
+        def _():
+            add_cores(n - 1)
+
+        @pl.when(jnp.logical_and(n >= 2, n < events + 2))
+        def _():
+            add_first(n - 2)
+
+        for at, stage in enumerate(stages):
+            since = n - planes - LAG - at
+            c = jnp.maximum(since, 0) // planes
+
+            @pl.when(jnp.logical_and(jnp.logical_and(since >= 0, c < parts), since % planes == 0))
+            def _():
+                stage(c)
+
+        return 0
+
+    lax.fori_loop(0, events + LAG + len(stages), event, 0)
 
     def drain(n, _):
         c, q = n // planes, n % planes
@@ -385,37 +414,23 @@
     columns, depth = integrals.shape
     tile = columns // tiles
     all_tiles = mirror_rows.shape[0] // tile
-    count = all_tiles // 2
-    per_plane = count // planes
+    per_plane = all_tiles // 2 // planes
     rows = amplitudes.shape[0] // (CORES * PARTS)
-
-    mask = (sym_rows[:, None] == jnp.repeat(sym_cols, tile)[None, :]).astype(jnp.bfloat16)
-    twin = mirror_rows.reshape(all_tiles, tile)
-    partner = twin[:, 0] // tile
-    here = jnp.arange(all_tiles, dtype=jnp.int32)
-    leads = here < partner
-    first = jnp.minimum(here, partner)
-    rank = jnp.sum((leads[None, :]) & (here[None, :] < first[:, None]), axis=1).astype(jnp.int32)
-    start = lax.axis_index("pair") * tiles
-    own_twin = lax.dynamic_slice_in_dim(twin, start, tiles, 0) % tile
-    own_leads = lax.dynamic_slice_in_dim(leads, start, tiles, 0)
-    own_rank = lax.dynamic_slice_in_dim(rank, start, tiles, 0)
-    lane = jnp.arange(tile, dtype=jnp.int32)
-    spot = jnp.where(own_leads[:, None], lane[None, :], own_twin)
-    sign = jnp.where(own_leads, 1.0, -1.0).astype(jnp.bfloat16)
-    turn = jnp.where(lane[None, :, None] == spot[:, None, :], sign[:, None, None], jnp.zeros((), jnp.bfloat16))
-    pick = (jnp.arange(count, dtype=jnp.int32)[:, None] == own_rank[None, :]).astype(jnp.float32).reshape(-1)
 
     dma = pltpu.SemaphoreType.DMA
     grid = (planes, PARTS)
     vmem = pl.BlockSpec(memory_space=pltpu.VMEM)
+    smem = pl.BlockSpec(memory_space=pltpu.SMEM)
+    hbm = pl.BlockSpec(memory_space=pl.ANY)
     group = per_plane * tile
     return pl.pallas_call(
         functools.partial(ladder_kernel, planes, tiles, tile),
         out_shape=jax.ShapeDtypeStruct((PARTS * rows, columns), jnp.bfloat16),
-        in_specs=[vmem, pl.BlockSpec(memory_space=pl.ANY), vmem, vmem, pl.BlockSpec(memory_space=pltpu.SMEM)],
+        in_specs=[hbm, hbm, smem, smem, smem, vmem],
         out_specs=vmem,
         scratch_shapes=[
+            pltpu.SMEM((tiles,), jnp.int32),
+            pltpu.VMEM((tiles, tile, tile), jnp.bfloat16),
             pltpu.VMEM((columns, depth), jnp.bfloat16),
             pltpu.VMEM((columns, depth), jnp.bfloat16),
             pltpu.VMEM((planes, CORES, PARTS, rows, depth), jnp.bfloat16),
@@ -427,7 +442,7 @@
             pltpu.VMEM((planes, PARTS, rows, group), jnp.float32),
             pltpu.VMEM((planes, PARTS, rows, group), jnp.float32),
             pltpu.VMEM((planes, PARTS, rows, group), jnp.bfloat16),
-            dma,
+            dma, dma,
             dma(grid), dma(grid), dma(grid), dma(grid), dma(grid),
             dma(grid), dma(grid), dma(grid), dma(grid),
             dma((PARTS,)), dma((PARTS,)), dma((PARTS,)), dma((PARTS,)),
@@ -441,7 +456,8 @@
             flops=2 * planes * amplitudes.shape[0] * columns * depth,
             bytes_accessed=2 * (amplitudes.size + integrals.size), transcendentals=0,
         ),
-    )(amplitudes.reshape(CORES, PARTS, rows, depth), integrals, mask, turn, pick)
+    )(amplitudes.reshape(CORES, PARTS, rows, depth), integrals, sym_rows, sym_cols,
+      mirror_rows, mirror_rows.reshape(all_tiles, tile))
 
 
 def solution(mesh):

time: 124 us -> 129 us (1.040)
  Pallas kernels: 117 us -> 123 us
  other arithmetic: 2.76 us -> 0 us
  local copies, waits for them, and re-layouts: 3.71 us -> 5.5 us
    pallas_call x1, Pallas kernels: 117 us -> 123 us  [shards(): pl.pallas_call(functools.partial(ladder_kernel, planes, tiles, tile), out...]
    unnamed x7 -> x11, local copies, waits for them, and re-layouts: 3.47 us -> 5.5 us
where the time goes in v2:
time: 129 us
  Pallas kernels  123 us (95%)
  local copies, waits for them, and re-layouts  5.5 us (4%)
    pallas_call x1, Pallas kernels, shards(): pl.pallas_call(functools.partial(ladder_kernel, planes, tiles, tile), out...  123 us
    unnamed x11, local copies, waits for them, and re-layouts  5.5 us

profile of v2, /device:TPU:0, one launch (start us, length us, event | category | flops | bytes accessed | tf_op | source)
XLA Modules:
  0.0 128.9 jit_solution(15627038785961269712)
XLA Ops:
  0.0 0.0 copy-start
  0.0 1.6 %copy-done = bf16[1024,1024]{1,0:T(8,128)(2,1)S(1)} copy-done((bf16[1024,1024]{1,0:T(8,128)(2,1)S(1)}, bf16[1024,1024]{1,0:T(8,128)(2,1)}, u32[]{:S(2)}) %copy-start) | copy-done | bytes 2097176
  1.6 0.0 copy-start.1
  1.6 1.1 copy-done.1
  2.7 0.0 copy-start.2
  2.7 0.7 copy-done.2
  3.4 0.0 copy-start.3
  3.4 0.7 copy-done.3
  4.1 0.0 copy-start.4
  4.1 0.7 copy-done.4
  4.8 123.4 %shard_map.55 = bf16[192,1024]{1,0:T(8,128)(2,1)S(1)} custom-call(bf16[2,4,48,1024]{3,2,1,0:T(8,128)(2,1)S(1)} %bitcast.2, bf16[1024,1024]{1,0:T(8,128)(2,1)S(1)} %copy-done, s32[8]{0:T(128)S(1)} %copy-done.3, s32[8]{0:T(128)S(1)} %copy-done.4, s32[4096]{0:T(1024)S(1)} %copy-done.2, s32[32,128]{1,0:T(8,128)S(1)} %bitcast.3), custom_call_target="tpu_custom_call" | custom-call | flops 3221225472 | bytes 2883584 | tf_op jit(solution)/shard_map/pallas_call | solution.py:426
  128.1 0.7 copy.7
Async XLA Ops:
  0.0 1.6 %copy-start = (bf16[1024,1024]{1,0:T(8,128)(2,1)S(1)}, bf16[1024,1024]{1,0:T(8,128)(2,1)}, u32[]{:S(2)}) copy-start(bf16[1024,1024]{1,0:T(8,128)(2,1)} %v_ref.1) | copy-start | bytes 6291460
  1.6 1.1 copy-start.1
  2.7 0.7 copy-start.2
  3.4 0.7 copy-start.3
  4.1 0.7 copy-start.4

commit v3 on v2

--- a/solution.py
+++ b/solution.py
@@ -10,6 +10,7 @@
 MESH = pl.DeviceIdType.MESH
 PARTS = 4
 LAG = 3
+AHEAD = 2
 CORES = 2
 SIDE = 2
 
@@ -103,7 +104,8 @@
         def _():
             t_copy(t_ref.at[:, c], p, c, t_left, p - 1).start()
 
-    own_t(0)
+    for c in range(AHEAD):
+        own_t(c)
 
     all_tiles = planes * tiles
     base = p * tiles
@@ -129,9 +131,9 @@
             keep = jnp.where(rows_ref[t] == cols_ref[u], 1.0, 0.0)
             lanes = slice(u * tile, (u + 1) * tile)
             v_in[span, lanes] = (v_in[span, lanes].astype(jnp.float32) * keep).astype(jnp.bfloat16)
-        turned[span, :] = jnp.dot(
+        turned[:, span] = jnp.dot(
             turn[t], v_in[span, :], preferred_element_type=jnp.float32
-        ).astype(jnp.bfloat16)
+        ).T.astype(jnp.bfloat16)
         return 0
 
     lax.fori_loop(0, tiles, prepare, 0)
@@ -177,16 +179,18 @@
             def _():
                 t_copy(tall.at[q, :, c], q, c, t_left, p - 1).start()
 
-        @pl.when(jnp.logical_and(at == 1, c + 1 < parts))
-        def _():
-            own_t(c + 1)
+        @pl.when(jnp.logical_and(at == 1, c + AHEAD < parts))
+        def _():
+            own_t(c + AHEAD)
 
         left = tall[q, :, c].reshape(CORES * rows, depth)
         wide = min(256, columns)
 
         def block(i, _):
             span = pl.ds(pl.multiple_of(i * wide, wide), wide)
-            prod[q, :, c, :, span] = contract_pair(left, turned[span, :]).reshape(CORES, rows, wide)
+            prod[q, :, c, :, span] = jnp.dot(
+                left, turned[:, span], preferred_element_type=jnp.float32
+            ).reshape(CORES, rows, wide)
             return 0
 
         lax.fori_loop(0, columns // wide, block, 0)
@@ -432,7 +436,7 @@
             pltpu.SMEM((tiles,), jnp.int32),
             pltpu.VMEM((tiles, tile, tile), jnp.bfloat16),
             pltpu.VMEM((columns, depth), jnp.bfloat16),
-            pltpu.VMEM((columns, depth), jnp.bfloat16),
+            pltpu.VMEM((depth, columns), jnp.bfloat16),
             pltpu.VMEM((planes, CORES, PARTS, rows, depth), jnp.bfloat16),
             pltpu.VMEM((planes, CORES, PARTS, rows, columns), jnp.float32),
             pltpu.VMEM((planes, PARTS, rows, columns), jnp.float32),

time: 129 us -> 130 us (level)
  no operation moved by 1% of the time
where the time goes in v3:
time: 130 us
  Pallas kernels  124 us (95%)
  local copies, waits for them, and re-layouts  5.5 us (4%)
    pallas_call x1, Pallas kernels, shards(): pl.pallas_call(functools.partial(ladder_kernel, planes, tiles, tile), out...  124 us
    unnamed x11, local copies, waits for them, and re-layouts  5.5 us

profile of v3, /device:TPU:0, one launch (start us, length us, event | category | flops | bytes accessed | tf_op | source)
XLA Modules:
  0.0 129.5 jit_solution(10995995912337792113)
XLA Ops:
  0.0 0.0 copy-start
  0.0 1.6 %copy-done = bf16[1024,1024]{1,0:T(8,128)(2,1)S(1)} copy-done((bf16[1024,1024]{1,0:T(8,128)(2,1)S(1)}, bf16[1024,1024]{1,0:T(8,128)(2,1)}, u32[]{:S(2)}) %copy-start) | copy-done | bytes 2097176
  1.6 0.0 copy-start.1
  1.6 1.1 copy-done.1
  2.7 0.0 copy-start.2
  2.7 0.7 copy-done.2
  3.4 0.0 copy-start.3
  3.4 0.7 copy-done.3
  4.1 0.0 copy-start.4
  4.1 0.7 copy-done.4
  4.8 124.0 %shard_map.55 = bf16[192,1024]{1,0:T(8,128)(2,1)S(1)} custom-call(bf16[2,4,48,1024]{3,2,1,0:T(8,128)(2,1)S(1)} %bitcast.2, bf16[1024,1024]{1,0:T(8,128)(2,1)S(1)} %copy-done, s32[8]{0:T(128)S(1)} %copy-done.3, s32[8]{0:T(128)S(1)} %copy-done.4, s32[4096]{0:T(1024)S(1)} %copy-done.2, s32[32,128]{1,0:T(8,128)S(1)} %bitcast.3), custom_call_target="tpu_custom_call" | custom-call | flops 3221225472 | bytes 2883584 | tf_op jit(solution)/shard_map/pallas_call | solution.py:430
  128.8 0.7 copy.7
Async XLA Ops:
  0.0 1.6 %copy-start = (bf16[1024,1024]{1,0:T(8,128)(2,1)S(1)}, bf16[1024,1024]{1,0:T(8,128)(2,1)}, u32[]{:S(2)}) copy-start(bf16[1024,1024]{1,0:T(8,128)(2,1)} %v_ref.1) | copy-start | bytes 6291460
  1.6 1.1 copy-start.1
  2.7 0.7 copy-start.2
  3.4 0.7 copy-start.3
  4.1 0.7 copy-start.4

commit v4 on v3

--- a/solution.py
+++ b/solution.py
@@ -9,7 +9,8 @@
 
 MESH = pl.DeviceIdType.MESH
 PARTS = 4
-LAG = 3
+LAG = 4
+SPACE = 2
 AHEAD = 2
 CORES = 2
 SIDE = 2
@@ -354,12 +355,12 @@
         def _():
             add_cores(n - 1)
 
-        @pl.when(jnp.logical_and(n >= 2, n < events + 2))
-        def _():
-            add_first(n - 2)
+        @pl.when(jnp.logical_and(n >= 1 + SPACE, n < events + 1 + SPACE))
+        def _():
+            add_first(n - 1 - SPACE)
 
         for at, stage in enumerate(stages):
-            since = n - planes - LAG - at
+            since = n - planes - LAG - at * SPACE
             c = jnp.maximum(since, 0) // planes
 
             @pl.when(jnp.logical_and(jnp.logical_and(since >= 0, c < parts), since % planes == 0))
@@ -368,7 +369,7 @@
 
         return 0
 
-    lax.fori_loop(0, events + LAG + len(stages), event, 0)
+    lax.fori_loop(0, events + LAG + SPACE * len(stages), event, 0)
 
     def drain(n, _):
         c, q = n // planes, n % planes

time: 130 us -> 116 us (0.89)
  Pallas kernels: 124 us -> 111 us
    pallas_call x1, Pallas kernels: 124 us -> 111 us  [shards(): pl.pallas_call(functools.partial(ladder_kernel, planes, tiles, tile), out...]
where the time goes in v4:
time: 116 us
  Pallas kernels  111 us (96%)
  local copies, waits for them, and re-layouts  5.5 us (5%)
    pallas_call x1, Pallas kernels, shards(): pl.pallas_call(functools.partial(ladder_kernel, planes, tiles, tile), out...  111 us
    unnamed x11, local copies, waits for them, and re-layouts  5.5 us

profile of v4, /device:TPU:0, one launch (start us, length us, event | category | flops | bytes accessed | tf_op | source)
XLA Modules:
  0.0 116.1 jit_solution(6058789675011367729)
XLA Ops:
  0.0 0.0 copy-start
  0.0 1.6 %copy-done = bf16[1024,1024]{1,0:T(8,128)(2,1)S(1)} copy-done((bf16[1024,1024]{1,0:T(8,128)(2,1)S(1)}, bf16[1024,1024]{1,0:T(8,128)(2,1)}, u32[]{:S(2)}) %copy-start) | copy-done | bytes 2097176
  1.6 0.0 copy-start.1
  1.6 1.1 copy-done.1
  2.7 0.0 copy-start.2
  2.7 0.7 copy-done.2
  3.4 0.0 copy-start.3
  3.4 0.7 copy-done.3
  4.1 0.0 copy-start.4
  4.1 0.7 copy-done.4
  4.8 110.6 %shard_map.55 = bf16[192,1024]{1,0:T(8,128)(2,1)S(1)} custom-call(bf16[2,4,48,1024]{3,2,1,0:T(8,128)(2,1)S(1)} %bitcast.2, bf16[1024,1024]{1,0:T(8,128)(2,1)S(1)} %copy-done, s32[8]{0:T(128)S(1)} %copy-done.3, s32[8]{0:T(128)S(1)} %copy-done.4, s32[4096]{0:T(1024)S(1)} %copy-done.2, s32[32,128]{1,0:T(8,128)S(1)} %bitcast.3), custom_call_target="tpu_custom_call" | custom-call | flops 3221225472 | bytes 2883584 | tf_op jit(solution)/shard_map/pallas_call | solution.py:431
  115.4 0.7 copy.7
Async XLA Ops:
  0.0 1.6 %copy-start = (bf16[1024,1024]{1,0:T(8,128)(2,1)S(1)}, bf16[1024,1024]{1,0:T(8,128)(2,1)}, u32[]{:S(2)}) copy-start(bf16[1024,1024]{1,0:T(8,128)(2,1)} %v_ref.1) | copy-start | bytes 6291460
  1.6 1.1 copy-start.1
  2.7 0.7 copy-start.2
  3.4 0.7 copy-start.3
  4.1 0.7 copy-start.4

commit v5 on v4

--- a/solution.py
+++ b/solution.py
@@ -42,7 +42,7 @@
     rank_ref, turn, v_in, turned, tall, prod, from_core, hop_one, hop_two, cont, from_left, from_right, slots,
     v_sem, own_sem, t_recv, t_right, t_left, core_send, core_recv,
     a_send, a_recv, b_send, b_recv, a2_send, a2_recv, b2_send, b2_recv,
-    zr_send, zr_recv, zl_send, zl_recv, gr_send, gl_send, g_recv,
+    zr_send, zr_recv, zl_send, zl_recv, g_send, g_recv,
 ):
     parts, rows, depth = t_ref.shape[1], t_ref.shape[2], t_ref.shape[3]
     columns = prod.shape[-1]
@@ -76,16 +76,10 @@
     for peer in (sibling, x_peer, y_peer):
         pl.semaphore_signal(barrier, inc=1, device_id={"intg": peer}, device_id_type=MESH)
 
-    @pl.when(p > 0)
-    def _():
-        pl.semaphore_signal(barrier, inc=1, device_id={"pair": p - 1}, device_id_type=MESH)
-
-    @pl.when(p < last)
-    def _():
-        pl.semaphore_signal(barrier, inc=1, device_id={"pair": p + 1}, device_id_type=MESH)
-
-    ends = (p == 0).astype(jnp.int32) + (p == last).astype(jnp.int32)
-    pl.semaphore_wait(barrier, 5 - ends)
+    for away in range(1, planes):
+        pl.semaphore_signal(
+            barrier, inc=1, device_id={"pair": (p + away) % planes}, device_id_type=MESH)
+    pl.semaphore_wait(barrier, 3 + last)
 
     def remote(src, dst, send, recv, **where):
         return pltpu.make_async_remote_copy(
@@ -279,11 +273,8 @@
 
             left_sum(q, c).start()
 
-    def right_slot(q, c):
-        return remote(slots.at[q, c], slots.at[q, c], gr_send.at[q, c], g_recv.at[q, c], pair=p + 1)
-
-    def left_slot(q, c):
-        return remote(slots.at[q, c], slots.at[q, c], gl_send.at[q, c], g_recv.at[q, c], pair=p - 1)
+    def slot_copy(q, c, away, plane):
+        return remote(slots.at[q, c], slots.at[q, c], g_send.at[away, c], g_recv.at[q, c], pair=plane)
 
     def settle(c):
         @pl.when(p > 0)
@@ -298,34 +289,21 @@
 
         slots[p, c] = cont[p, c].astype(jnp.bfloat16)
 
-        @pl.when(p < last)
-        def _():
-            right_slot(p, c).start()
-
-        @pl.when(p > 0)
-        def _():
-            left_slot(p, c).start()
-
-    def pass_on(c, away):
-        @pl.when(p - away >= 0)
-        def _():
-            q = p - away
-            right_slot(q, c).wait_recv()
-
-            @pl.when(p < last)
-            def _():
-                right_slot(q, c).start()
-
-        @pl.when(p + away <= last)
-        def _():
-            q = p + away
-            left_slot(q, c).wait_recv()
-
-            @pl.when(p > 0)
-            def _():
-                left_slot(q, c).start()
+        for away in range(last, 0, -1):
+            @pl.when(p + away <= last)
+            def _():
+                slot_copy(p, c, away, p + away).start()
+
+            @pl.when(p - away >= 0)
+            def _():
+                slot_copy(p, c, planes - away, p - away).start()
 
     def emit(c):
+        for q in range(planes):
+            @pl.when(q != p)
+            def _():
+                slot_copy(q, c, 0, p).wait_recv()
+
         def one(t, _):
             total = jnp.zeros((rows, tile), jnp.float32)
             for q in range(planes):
@@ -343,7 +321,6 @@
     stages = [collect]
     stages += [functools.partial(send_sums, away=away) for away in range(last - 1, 0, -1)]
     stages += [settle]
-    stages += [functools.partial(pass_on, away=away) for away in range(1, planes)]
     stages += [emit]
 
     def event(n, _):
@@ -361,15 +338,17 @@
 
         for at, stage in enumerate(stages):
             since = n - planes - LAG - at * SPACE
-            c = jnp.maximum(since, 0) // planes
-
-            @pl.when(jnp.logical_and(jnp.logical_and(since >= 0, c < parts), since % planes == 0))
+            final = since == events - planes - LAG + SPACE
+            c = jnp.where(final, parts - 1, jnp.maximum(since, 0) // planes)
+            early = jnp.logical_and(jnp.logical_and(since >= 0, since % planes == 0), c < parts - 1)
+
+            @pl.when(jnp.logical_or(final, early))
             def _():
                 stage(c)
 
         return 0
 
-    lax.fori_loop(0, events + LAG + SPACE * len(stages), event, 0)
+    lax.fori_loop(0, events + 1 + SPACE * len(stages), event, 0)
 
     def drain(n, _):
         c, q = n // planes, n % planes
@@ -394,19 +373,19 @@
         @pl.when(jnp.logical_and(q <= p, p < last))
         def _():
             t_copy(tall.at[q, :, c], q, c, t_right, p + 1).wait_send()
-            right_slot(q, c).wait_send()
 
         @pl.when(jnp.logical_and(q >= p, p > 0))
         def _():
             t_copy(tall.at[q, :, c], q, c, t_left, p - 1).wait_send()
-            left_slot(q, c).wait_send()
 
         @pl.when(q > p)
         def _():
+            slot_copy(p, c, q - p, q).wait_send()
             right_sum(q, c).wait_send()
 
         @pl.when(q < p)
         def _():
+            slot_copy(p, c, planes - p + q, q).wait_send()
             left_sum(q, c).wait_send()
 
         return 0
@@ -452,10 +431,10 @@
             dma(grid), dma(grid), dma(grid), dma(grid),
             dma((PARTS,)), dma((PARTS,)), dma((PARTS,)), dma((PARTS,)),
             dma(grid), dma(grid), dma(grid), dma(grid),
-            dma(grid), dma(grid), dma(grid),
+            dma(grid), dma(grid),
         ],
         compiler_params=pltpu.CompilerParams(
-            collective_id=0, has_side_effects=True, vmem_limit_bytes=48 * 1024 * 1024
+            collective_id=0, has_side_effects=True, vmem_limit_bytes=60 * 1024 * 1024
         ),
         cost_estimate=pl.CostEstimate(
             flops=2 * planes * amplitudes.shape[0] * columns * depth,

time: 116 us -> 117 us (level)
  Pallas kernels: 111 us -> 115 us
  local copies, waits for them, and re-layouts: 5.5 us -> 1.77 us
    pallas_call x1, Pallas kernels: 111 us -> 115 us  [shards(): pl.pallas_call(functools.partial(ladder_kernel, planes, tiles, tile), out...]
    unnamed x11 -> x1, local copies, waits for them, and re-layouts: 5.5 us -> 1.77 us
where the time goes in v5:
time: 117 us; the launch traced here: 116 us
  Pallas kernels  115 us (98%)
  local copies, waits for them, and re-layouts  1.77 us (2%)
    pallas_call x1, Pallas kernels, shards(): pl.pallas_call(functools.partial(ladder_kernel, planes, tiles, tile), out...  115 us

profile of v5, /device:TPU:0, one launch (start us, length us, event | category | flops | bytes accessed | tf_op | source)
XLA Modules:
  0.0 116.5 jit_solution(6996609708164437184)
XLA Ops:
  0.0 114.7 %shard_map.55 = bf16[192,1024]{1,0:T(8,128)(2,1)} custom-call(bf16[2,4,48,1024]{3,2,1,0:T(8,128)(2,1)} %bitcast.2, bf16[1024,1024]{1,0:T(8,128)(2,1)} %v_ref.1, s32[8]{0:T(128)} %rows_ref.1, s32[8]{0:T(128)} %cols_ref.1, s32[4096]{0:T(1024)} %mirror_ref.1, s32[32,128]{1,0:T(8,128)} %bitcast.3), custom_call_target="tpu_custom_call" | custom-call | flops 3221225472 | bytes 2883584 | tf_op jit(solution)/shard_map/pallas_call | solution.py:410
  114.7 1.8 %copy.7 = bf16[192,1024]{1,0:T(8,128)(2,1)} copy(bf16[192,1024]{1,0:T(8,128)(2,1)} %shard_map.55) | data formatting | bytes 786432

commit v6 on v5

--- a/solution.py
+++ b/solution.py
@@ -11,6 +11,7 @@
 PARTS = 4
 LAG = 4
 SPACE = 2
+OWNERS = 2
 AHEAD = 2
 CORES = 2
 SIDE = 2
@@ -48,7 +49,7 @@
     columns = prod.shape[-1]
     half = columns // 2
     group = cont.shape[-1]
-    per_plane = group // tile
+    per_owner = group // tile
     last = planes - 1
     p = lax.axis_index("pair")
     g = lax.axis_index("intg")
@@ -243,72 +244,61 @@
             total = jnp.zeros((rows, tile), jnp.float32)
             for t in range(tiles):
                 total = total + pick(k, t) * prod[chip, core, c, :, t * tile : (t + 1) * tile]
-            span = pl.ds(pl.multiple_of(k % per_plane * tile, tile), tile)
-            cont[k // per_plane, c, :, span] = total
+            span = pl.ds(pl.multiple_of(k % per_owner * tile, tile), tile)
+            cont[k // per_owner, c, :, span] = total
             return 0
 
-        lax.fori_loop(0, planes * per_plane, fill, 0)
-        send_sums(c, last)
-
-    def send_sums(c, away):
-        @pl.when(p + away <= last)
-        def _():
-            q = p + away
-
-            @pl.when(p > 0)
-            def _():
-                right_sum(q, c).wait_recv()
-                cont[q, c] = cont[q, c] + from_left[q, c]
-
-            right_sum(q, c).start()
-
-        @pl.when(p - away >= 0)
-        def _():
-            q = p - away
-
-            @pl.when(p < last)
-            def _():
-                left_sum(q, c).wait_recv()
-                cont[q, c] = cont[q, c] + from_right[q, c]
-
-            left_sum(q, c).start()
+        lax.fori_loop(0, OWNERS * per_owner, fill, 0)
+
+        @pl.when(p == 0)
+        def _():
+            right_sum(1, c).start()
+            right_sum(0, c).start()
+
+        @pl.when(p == last)
+        def _():
+            left_sum(0, c).start()
+            left_sum(1, c).start()
+
+    def send_on(c):
+        @pl.when(p == 1)
+        def _():
+            right_sum(1, c).wait_recv()
+            cont[1, c] = cont[1, c] + from_left[1, c]
+            right_sum(1, c).start()
+
+        @pl.when(p == 2)
+        def _():
+            left_sum(0, c).wait_recv()
+            cont[0, c] = cont[0, c] + from_right[0, c]
+            left_sum(0, c).start()
 
     def slot_copy(q, c, away, plane):
         return remote(slots.at[q, c], slots.at[q, c], g_send.at[away, c], g_recv.at[q, c], pair=plane)
 
+    inner = jnp.logical_and(p > 0, p < last)
+    own = jnp.clip(p - 1, 0, OWNERS - 1)
+
     def settle(c):
-        @pl.when(p > 0)
-        def _():
-            right_sum(p, c).wait_recv()
-            cont[p, c] = cont[p, c] + from_left[p, c]
-
-        @pl.when(p < last)
-        def _():
-            left_sum(p, c).wait_recv()
-            cont[p, c] = cont[p, c] + from_right[p, c]
-
-        slots[p, c] = cont[p, c].astype(jnp.bfloat16)
-
-        for away in range(last, 0, -1):
-            @pl.when(p + away <= last)
-            def _():
-                slot_copy(p, c, away, p + away).start()
-
-            @pl.when(p - away >= 0)
-            def _():
-                slot_copy(p, c, planes - away, p - away).start()
+        @pl.when(inner)
+        def _():
+            right_sum(own, c).wait_recv()
+            left_sum(own, c).wait_recv()
+            slots[own, c] = (cont[own, c] + from_left[own, c] + from_right[own, c]).astype(jnp.bfloat16)
+            for away in range(1, planes):
+                slot_copy(own, c, away, (p + away) % planes).start()
 
     def emit(c):
-        for q in range(planes):
-            @pl.when(q != p)
+        for q in range(OWNERS):
+            @pl.when(p != q + 1)
             def _():
                 slot_copy(q, c, 0, p).wait_recv()
 
         def one(t, _):
             total = jnp.zeros((rows, tile), jnp.float32)
-            for q in range(planes):
-                for s in range(per_plane):
-                    scale = pick(q * per_plane + s, t)
+            for q in range(OWNERS):
+                for s in range(per_owner):
+                    scale = pick(q * per_owner + s, t)
                     total = total + scale * slots[q, c, :, s * tile : (s + 1) * tile].astype(jnp.float32)
             span = pl.ds(pl.multiple_of(t * tile, tile), tile)
             out_ref[pl.ds(pl.multiple_of(c * rows, rows), rows), span] = jnp.dot(
@@ -318,10 +308,7 @@
 
         lax.fori_loop(0, tiles, one, 0)
 
-    stages = [collect]
-    stages += [functools.partial(send_sums, away=away) for away in range(last - 1, 0, -1)]
-    stages += [settle]
-    stages += [emit]
+    stages = [collect, send_on, settle, emit]
 
     def event(n, _):
         @pl.when(n < events)
@@ -378,15 +365,25 @@
         def _():
             t_copy(tall.at[q, :, c], q, c, t_left, p - 1).wait_send()
 
-        @pl.when(q > p)
-        def _():
-            slot_copy(p, c, q - p, q).wait_send()
+        @pl.when(jnp.logical_and(q < OWNERS, p == 0))
+        def _():
             right_sum(q, c).wait_send()
 
-        @pl.when(q < p)
-        def _():
-            slot_copy(p, c, planes - p + q, q).wait_send()
+        @pl.when(jnp.logical_and(q < OWNERS, p == last))
+        def _():
             left_sum(q, c).wait_send()
+
+        @pl.when(jnp.logical_and(q == 1, p == 1))
+        def _():
+            right_sum(q, c).wait_send()
+
+        @pl.when(jnp.logical_and(q == 0, p == 2))
+        def _():
+            left_sum(q, c).wait_send()
+
+        @pl.when(jnp.logical_and(inner, q > 0))
+        def _():
+            slot_copy(own, c, q, p).wait_send()
 
         return 0
 
@@ -398,7 +395,7 @@
     columns, depth = integrals.shape
     tile = columns // tiles
     all_tiles = mirror_rows.shape[0] // tile
-    per_plane = all_tiles // 2 // planes
+    per_owner = all_tiles // 2 // OWNERS
     rows = amplitudes.shape[0] // (CORES * PARTS)
 
     dma = pltpu.SemaphoreType.DMA
@@ -406,7 +403,7 @@
     vmem = pl.BlockSpec(memory_space=pltpu.VMEM)
     smem = pl.BlockSpec(memory_space=pltpu.SMEM)
     hbm = pl.BlockSpec(memory_space=pl.ANY)
-    group = per_plane * tile
+    group = per_owner * tile
     return pl.pallas_call(
         functools.partial(ladder_kernel, planes, tiles, tile),
         out_shape=jax.ShapeDtypeStruct((PARTS * rows, columns), jnp.bfloat16),
@@ -422,10 +419,10 @@
             pltpu.VMEM((planes, PARTS, rows, columns), jnp.float32),
             pltpu.VMEM((planes, PARTS, rows, columns), jnp.float32),
             pltpu.VMEM((PARTS, rows, columns), jnp.float32),
-            pltpu.VMEM((planes, PARTS, rows, group), jnp.float32),
-            pltpu.VMEM((planes, PARTS, rows, group), jnp.float32),
-            pltpu.VMEM((planes, PARTS, rows, group), jnp.float32),
-            pltpu.VMEM((planes, PARTS, rows, group), jnp.bfloat16),
+            pltpu.VMEM((OWNERS, PARTS, rows, group), jnp.float32),
+            pltpu.VMEM((OWNERS, PARTS, rows, group), jnp.float32),
+            pltpu.VMEM((OWNERS, PARTS, rows, group), jnp.float32),
+            pltpu.VMEM((OWNERS, PARTS, rows, group), jnp.bfloat16),
             dma, dma,
             dma(grid), dma(grid), dma(grid), dma(grid), dma(grid),
             dma(grid), dma(grid), dma(grid), dma(grid),

time: 117 us -> 110 us (0.940)
  Pallas kernels: 115 us -> 108 us
    pallas_call x1, Pallas kernels: 115 us -> 108 us  [shards(): pl.pallas_call(functools.partial(ladder_kernel, planes, tiles, tile), out...]
where the time goes in v6:
time: 110 us
  Pallas kernels  108 us (98%)
  local copies, waits for them, and re-layouts  1.77 us (2%)
    pallas_call x1, Pallas kernels, shards(): pl.pallas_call(functools.partial(ladder_kernel, planes, tiles, tile), out...  108 us

profile of v6, /device:TPU:0, one launch (start us, length us, event | category | flops | bytes accessed | tf_op | source)
XLA Modules:
  0.0 110.1 jit_solution(17888703634988574387)
XLA Ops:
  0.0 108.4 %shard_map.55 = bf16[192,1024]{1,0:T(8,128)(2,1)} custom-call(bf16[2,4,48,1024]{3,2,1,0:T(8,128)(2,1)} %bitcast.2, bf16[1024,1024]{1,0:T(8,128)(2,1)} %v_ref.1, s32[8]{0:T(128)} %rows_ref.1, s32[8]{0:T(128)} %cols_ref.1, s32[4096]{0:T(1024)} %mirror_ref.1, s32[32,128]{1,0:T(8,128)} %bitcast.3), custom_call_target="tpu_custom_call" | custom-call | flops 3221225472 | bytes 2883584 | tf_op jit(solution)/shard_map/pallas_call | solution.py:407
  108.4 1.8 %copy.7 = bf16[192,1024]{1,0:T(8,128)(2,1)} copy(bf16[192,1024]{1,0:T(8,128)(2,1)} %shard_map.55) | data formatting | bytes 786432

commit v7 on v6

--- a/solution.py
+++ b/solution.py
@@ -40,10 +40,10 @@
 def ladder_kernel(
     planes, tiles, tile,
     t_ref, v_ref, rows_ref, cols_ref, mirror_ref, twin_ref, out_ref,
-    rank_ref, turn, v_in, turned, tall, prod, from_core, hop_one, hop_two, cont, from_left, from_right, slots,
+    rank_ref, turn, v_in, turned, tall, prod, from_core, hop_one, hop_two, cont, from_left, from_right, slots, packs, landed,
     v_sem, own_sem, t_recv, t_right, t_left, core_send, core_recv,
     a_send, a_recv, b_send, b_recv, a2_send, a2_recv, b2_send, b2_recv,
-    zr_send, zr_recv, zl_send, zl_recv, g_send, g_recv,
+    zr_send, zr_recv, zl_send, zl_recv, pack_send, land_recv,
 ):
     parts, rows, depth = t_ref.shape[1], t_ref.shape[2], t_ref.shape[3]
     columns = prod.shape[-1]
@@ -105,18 +105,12 @@
 
     all_tiles = planes * tiles
     base = p * tiles
-    partners = [mirror_ref[u * tile] // tile for u in range(all_tiles)]
     load_v.wait()
 
     def prepare(t, _):
         at = base + t
         partner = mirror_ref[at * tile] // tile
         leads = at < partner
-        first = jnp.minimum(at, partner)
-        rank = jnp.int32(0)
-        for u in range(all_tiles):
-            rank = rank + jnp.where(jnp.logical_and(u < partners[u], u < first), 1, 0)
-        rank_ref[t] = rank
         lane = lax.broadcasted_iota(jnp.int32, (1, tile), 1)
         spot = jnp.where(leads, lane, twin_ref[pl.ds(at, 1), :] - partner * tile)
         sign = jnp.where(leads, 1.0, -1.0)
@@ -133,6 +127,20 @@
         return 0
 
     lax.fori_loop(0, tiles, prepare, 0)
+
+    def rank_all():
+        partners = [mirror_ref[u * tile] // tile for u in range(all_tiles)]
+
+        def one(at, _):
+            first = jnp.minimum(at, mirror_ref[at * tile] // tile)
+            rank = jnp.int32(0)
+            for u in range(all_tiles):
+                rank = rank + jnp.where(jnp.logical_and(u < partners[u], u < first), 1, 0)
+            rank_ref[at] = rank
+            return 0
+
+        lax.fori_loop(0, all_tiles, one, 0)
+
     load_t.wait()
 
     def core_copy(q, c):
@@ -243,7 +251,7 @@
         def fill(k, _):
             total = jnp.zeros((rows, tile), jnp.float32)
             for t in range(tiles):
-                total = total + pick(k, t) * prod[chip, core, c, :, t * tile : (t + 1) * tile]
+                total = total + pick(k, base + t) * prod[chip, core, c, :, t * tile : (t + 1) * tile]
             span = pl.ds(pl.multiple_of(k % per_owner * tile, tile), tile)
             cont[k // per_owner, c, :, span] = total
             return 0
@@ -273,47 +281,72 @@
             cont[0, c] = cont[0, c] + from_right[0, c]
             left_sum(0, c).start()
 
-    def slot_copy(q, c, away, plane):
-        return remote(slots.at[q, c], slots.at[q, c], g_send.at[away, c], g_recv.at[q, c], pair=plane)
-
     inner = jnp.logical_and(p > 0, p < last)
     own = jnp.clip(p - 1, 0, OWNERS - 1)
 
+    peer = last - p
+    end = jnp.where(p == 1, 0, last)
+
+    def peer_copy(i, c):
+        return remote(packs.at[i, c], landed.at[i, c], pack_send.at[i, c], land_recv.at[i, c], pair=peer)
+
+    def end_copy(c):
+        return remote(packs.at[2, c], landed.at[0, c], pack_send.at[2, c], land_recv.at[0, c], pair=end)
+
     def settle(c):
         @pl.when(inner)
         def _():
             right_sum(own, c).wait_recv()
             left_sum(own, c).wait_recv()
-            slots[own, c] = (cont[own, c] + from_left[own, c] + from_right[own, c]).astype(jnp.bfloat16)
-            for away in range(1, planes):
-                slot_copy(own, c, away, (p + away) % planes).start()
+            slots[c] = (cont[own, c] + from_left[own, c] + from_right[own, c]).astype(jnp.bfloat16)
+
+            def pack(t, _):
+                span = pl.ds(pl.multiple_of(t * tile, tile), tile)
+                for i, plane in enumerate((peer, last - end, end, p)):
+                    total = jnp.zeros((rows, tile), jnp.float32)
+                    for s in range(per_owner):
+                        scale = pick(own * per_owner + s, plane * tiles + t)
+                        total = total + scale * slots[c, :, s * tile : (s + 1) * tile].astype(jnp.float32)
+                    packs[i, c, :, span] = total.astype(jnp.bfloat16)
+                return 0
+
+            lax.fori_loop(0, tiles, pack, 0)
+            peer_copy(1, c).start()
+            peer_copy(0, c).start()
+
+    def merge(c):
+        @pl.when(inner)
+        def _():
+            peer_copy(1, c).wait_recv()
+            packs[2, c] = packs[2, c] + landed[1, c]
+            end_copy(c).start()
 
     def emit(c):
-        for q in range(OWNERS):
-            @pl.when(p != q + 1)
-            def _():
-                slot_copy(q, c, 0, p).wait_recv()
+        end_copy(c).wait_recv()
+
+        @pl.when(inner)
+        def _():
+            landed[0, c] = landed[0, c] + packs[3, c]
 
         def one(t, _):
-            total = jnp.zeros((rows, tile), jnp.float32)
-            for q in range(OWNERS):
-                for s in range(per_owner):
-                    scale = pick(q * per_owner + s, t)
-                    total = total + scale * slots[q, c, :, s * tile : (s + 1) * tile].astype(jnp.float32)
             span = pl.ds(pl.multiple_of(t * tile, tile), tile)
             out_ref[pl.ds(pl.multiple_of(c * rows, rows), rows), span] = jnp.dot(
-                total.astype(jnp.bfloat16), turn[t], preferred_element_type=jnp.float32
+                landed[0, c, :, span], turn[t], preferred_element_type=jnp.float32
             ).astype(jnp.bfloat16)
             return 0
 
         lax.fori_loop(0, tiles, one, 0)
 
-    stages = [collect, send_on, settle, emit]
+    stages = [collect, send_on, settle, merge, emit]
 
     def event(n, _):
         @pl.when(n < events)
         def _():
             multiply(n)
+
+        @pl.when(n == 1)
+        def _():
+            rank_all()
 
         @pl.when(jnp.logical_and(n >= 1, n < events + 1))
         def _():
@@ -381,9 +414,13 @@
         def _():
             left_sum(q, c).wait_send()
 
-        @pl.when(jnp.logical_and(inner, q > 0))
-        def _():
-            slot_copy(own, c, q, p).wait_send()
+        @pl.when(jnp.logical_and(inner, q < 2))
+        def _():
+            peer_copy(q, c).wait_send()
+
+        @pl.when(jnp.logical_and(inner, q == 2))
+        def _():
+            end_copy(c).wait_send()
 
         return 0
 
@@ -410,7 +447,7 @@
         in_specs=[hbm, hbm, smem, smem, smem, vmem],
         out_specs=vmem,
         scratch_shapes=[
-            pltpu.SMEM((tiles,), jnp.int32),
+            pltpu.SMEM((all_tiles,), jnp.int32),
             pltpu.VMEM((tiles, tile, tile), jnp.bfloat16),
             pltpu.VMEM((columns, depth), jnp.bfloat16),
             pltpu.VMEM((depth, columns), jnp.bfloat16),
@@ -422,13 +459,15 @@
             pltpu.VMEM((OWNERS, PARTS, rows, group), jnp.float32),
             pltpu.VMEM((OWNERS, PARTS, rows, group), jnp.float32),
             pltpu.VMEM((OWNERS, PARTS, rows, group), jnp.float32),
-            pltpu.VMEM((OWNERS, PARTS, rows, group), jnp.bfloat16),
+            pltpu.VMEM((PARTS, rows, group), jnp.bfloat16),
+            pltpu.VMEM((4, PARTS, rows, columns), jnp.bfloat16),
+            pltpu.VMEM((2, PARTS, rows, columns), jnp.bfloat16),
             dma, dma,
             dma(grid), dma(grid), dma(grid), dma(grid), dma(grid),
             dma(grid), dma(grid), dma(grid), dma(grid),
             dma((PARTS,)), dma((PARTS,)), dma((PARTS,)), dma((PARTS,)),
             dma(grid), dma(grid), dma(grid), dma(grid),
-            dma(grid), dma(grid),
+            dma((3, PARTS)), dma((2, PARTS)),
         ],
         compiler_params=pltpu.CompilerParams(
             collective_id=0, has_side_effects=True, vmem_limit_bytes=60 * 1024 * 1024

time: 110 us -> 114 us (1.036)
  Pallas kernels: 108 us -> 112 us
    pallas_call x1, Pallas kernels: 108 us -> 112 us  [shards(): pl.pallas_call(functools.partial(ladder_kernel, planes, tiles, tile), out...]
where the time goes in v7:
time: 114 us
  Pallas kernels  112 us (98%)
  local copies, waits for them, and re-layouts  1.77 us (2%)
    pallas_call x1, Pallas kernels, shards(): pl.pallas_call(functools.partial(ladder_kernel, planes, tiles, tile), out...  112 us

profile of v7, /device:TPU:0, one launch (start us, length us, event | category | flops | bytes accessed | tf_op | source)
XLA Modules:
  0.0 114.0 jit_solution(14524860518524128695)
XLA Ops:
  0.0 112.2 %shard_map.55 = bf16[192,1024]{1,0:T(8,128)(2,1)} custom-call(bf16[2,4,48,1024]{3,2,1,0:T(8,128)(2,1)} %bitcast.2, bf16[1024,1024]{1,0:T(8,128)(2,1)} %v_ref.1, s32[8]{0:T(128)} %rows_ref.1, s32[8]{0:T(128)} %cols_ref.1, s32[4096]{0:T(1024)} %mirror_ref.1, s32[32,128]{1,0:T(8,128)} %bitcast.3), custom_call_target="tpu_custom_call" | custom-call | flops 3221225472 | bytes 2883584 | tf_op jit(solution)/shard_map/pallas_call | solution.py:444
  112.2 1.8 %copy.7 = bf16[192,1024]{1,0:T(8,128)(2,1)} copy(bf16[192,1024]{1,0:T(8,128)(2,1)} %shard_map.55) | data formatting | bytes 786432

commit v8 on v6

--- a/solution.py
+++ b/solution.py
@@ -8,11 +8,12 @@
 from jax.sharding import PartitionSpec as P
 
 MESH = pl.DeviceIdType.MESH
-PARTS = 4
+PARTS = 6
 LAG = 4
-SPACE = 2
+HOP = 2
+SPACE = 3
 OWNERS = 2
-AHEAD = 2
+AHEAD = 3
 CORES = 2
 SIDE = 2
 
@@ -319,9 +320,9 @@
         def _():
             add_cores(n - 1)
 
-        @pl.when(jnp.logical_and(n >= 1 + SPACE, n < events + 1 + SPACE))
-        def _():
-            add_first(n - 1 - SPACE)
+        @pl.when(jnp.logical_and(n >= 1 + HOP, n < events + 1 + HOP))
+        def _():
+            add_first(n - 1 - HOP)
 
         for at, stage in enumerate(stages):
             since = n - planes - LAG - at * SPACE

time: 110 us -> 107 us (0.973)
  Pallas kernels: 108 us -> 105 us
    pallas_call x1, Pallas kernels: 108 us -> 105 us  [shards(): pl.pallas_call(functools.partial(ladder_kernel, planes, tiles, tile), out...]
where the time goes in v8:
time: 107 us
  Pallas kernels  105 us (98%)
  local copies, waits for them, and re-layouts  1.77 us (2%)
    pallas_call x1, Pallas kernels, shards(): pl.pallas_call(functools.partial(ladder_kernel, planes, tiles, tile), out...  105 us

profile of v8, /device:TPU:0, one launch (start us, length us, event | category | flops | bytes accessed | tf_op | source)
XLA Modules:
  0.0 107.0 jit_solution(2052559140523106732)
XLA Ops:
  0.0 105.3 %shard_map.55 = bf16[192,1024]{1,0:T(8,128)(2,1)} custom-call(bf16[2,6,32,1024]{3,2,1,0:T(8,128)(2,1)} %bitcast.2, bf16[1024,1024]{1,0:T(8,128)(2,1)} %v_ref.1, s32[8]{0:T(128)} %rows_ref.1, s32[8]{0:T(128)} %cols_ref.1, s32[4096]{0:T(1024)} %mirror_ref.1, s32[32,128]{1,0:T(8,128)} %bitcast.3), custom_call_target="tpu_custom_call" | custom-call | flops 3221225472 | bytes 2883584 | tf_op jit(solution)/shard_map/pallas_call | solution.py:408
  105.3 1.8 %copy.7 = bf16[192,1024]{1,0:T(8,128)(2,1)} copy(bf16[192,1024]{1,0:T(8,128)(2,1)} %shard_map.55) | data formatting | bytes 786432

commit v9 on v8

--- a/solution.py
+++ b/solution.py
@@ -159,6 +159,17 @@
                       b2_send.at[c], b2_recv.at[c], intg=x_peer)
 
     events = planes * parts
+    wide = min(256, columns)
+
+    def own_block(i, _):
+        span = pl.ds(pl.multiple_of(i * wide, wide), wide)
+        prod[p, :, :, :, span] = jnp.dot(
+            tall[p].reshape(CORES * parts * rows, depth), turned[:, span],
+            preferred_element_type=jnp.float32,
+        ).reshape(CORES, parts, rows, wide)
+        return 0
+
+    lax.fori_loop(0, columns // wide, own_block, 0)
 
     def multiply(n):
         c, at = n // planes, n % planes
@@ -180,17 +191,19 @@
         def _():
             own_t(c + AHEAD)
 
-        left = tall[q, :, c].reshape(CORES * rows, depth)
-        wide = min(256, columns)
-
-        def block(i, _):
-            span = pl.ds(pl.multiple_of(i * wide, wide), wide)
-            prod[q, :, c, :, span] = jnp.dot(
-                left, turned[:, span], preferred_element_type=jnp.float32
-            ).reshape(CORES, rows, wide)
-            return 0
-
-        lax.fori_loop(0, columns // wide, block, 0)
+        @pl.when(at > 0)
+        def _():
+            left = tall[q, :, c].reshape(CORES * rows, depth)
+
+            def block(i, _):
+                span = pl.ds(pl.multiple_of(i * wide, wide), wide)
+                prod[q, :, c, :, span] = jnp.dot(
+                    left, turned[:, span], preferred_element_type=jnp.float32
+                ).reshape(CORES, rows, wide)
+                return 0
+
+            lax.fori_loop(0, columns // wide, block, 0)
+
         core_copy(q, c).start()
 
     def add_cores(n):

time: 107 us -> 107 us (level)
  no operation moved by 1% of the time
where the time goes in v9:
time: 107 us
  Pallas kernels  105 us (98%)
  local copies, waits for them, and re-layouts  1.77 us (2%)
    pallas_call x1, Pallas kernels, shards(): pl.pallas_call(functools.partial(ladder_kernel, planes, tiles, tile), out...  105 us

profile of v9, /device:TPU:0, one launch (start us, length us, event | category | flops | bytes accessed | tf_op | source)
XLA Modules:
  0.0 106.7 jit_solution(1062735487050931261)
XLA Ops:
  0.0 104.9 %shard_map.55 = bf16[192,1024]{1,0:T(8,128)(2,1)} custom-call(bf16[2,6,32,1024]{3,2,1,0:T(8,128)(2,1)} %bitcast.2, bf16[1024,1024]{1,0:T(8,128)(2,1)} %v_ref.1, s32[8]{0:T(128)} %rows_ref.1, s32[8]{0:T(128)} %cols_ref.1, s32[4096]{0:T(1024)} %mirror_ref.1, s32[32,128]{1,0:T(8,128)} %bitcast.3), custom_call_target="tpu_custom_call" | custom-call | flops 3221225472 | bytes 2883584 | tf_op jit(solution)/shard_map/pallas_call | solution.py:421
  104.9 1.8 %copy.7 = bf16[192,1024]{1,0:T(8,128)(2,1)} copy(bf16[192,1024]{1,0:T(8,128)(2,1)} %shard_map.55) | data formatting | bytes 786432

commit v10 on v9

--- a/solution.py
+++ b/solution.py
@@ -9,7 +9,7 @@
 
 MESH = pl.DeviceIdType.MESH
 PARTS = 6
-LAG = 4
+LAG = 3
 HOP = 2
 SPACE = 3
 OWNERS = 2

time: 107 us -> 109 us (1.019)
  Pallas kernels: 105 us -> 107 us
    pallas_call x1, Pallas kernels: 105 us -> 107 us  [shards(): pl.pallas_call(functools.partial(ladder_kernel, planes, tiles, tile), out...]
where the time goes in v10:
time: 109 us
  Pallas kernels  107 us (98%)
  local copies, waits for them, and re-layouts  1.77 us (2%)
    pallas_call x1, Pallas kernels, shards(): pl.pallas_call(functools.partial(ladder_kernel, planes, tiles, tile), out...  107 us

profile of v10, /device:TPU:0, one launch (start us, length us, event | category | flops | bytes accessed | tf_op | source)
XLA Modules:
  0.0 109.0 jit_solution(12851242608599402647)
XLA Ops:
  0.0 107.2 %shard_map.55 = bf16[192,1024]{1,0:T(8,128)(2,1)} custom-call(bf16[2,6,32,1024]{3,2,1,0:T(8,128)(2,1)} %bitcast.2, bf16[1024,1024]{1,0:T(8,128)(2,1)} %v_ref.1, s32[8]{0:T(128)} %rows_ref.1, s32[8]{0:T(128)} %cols_ref.1, s32[4096]{0:T(1024)} %mirror_ref.1, s32[32,128]{1,0:T(8,128)} %bitcast.3), custom_call_target="tpu_custom_call" | custom-call | flops 3221225472 | bytes 2883584 | tf_op jit(solution)/shard_map/pallas_call | solution.py:421
  107.3 1.8 %copy.7 = bf16[192,1024]{1,0:T(8,128)(2,1)} copy(bf16[192,1024]{1,0:T(8,128)(2,1)} %shard_map.55) | data formatting | bytes 786432
